TPU v7x, 32 devices: a whole 2x2x4 slice. The times are simulated.
32 devices in a mesh: groups: 2 (over x), seq: 16 (over z, y, core).
Axes of the slice: x: 2, y: 2, z: 4, core: 2. Of those that a mesh axis runs over, the one named last changes fastest.
Arguments:
- tokens: bfloat16 [8192, 256], P(('groups', 'seq')), parts along dimension 0, may hold values from -6 to 6
- norm_gain: float32 [256], replicated, may hold values from 0.1 to 1.9
- w_in: bfloat16 [256, 768], replicated, may hold values from -0.375 to 0.375
- short_filter: float32 [3, 768], replicated, may hold values from -0.8 to 0.8
- long_filter: float32 [4096, 256], P('seq'), may hold values from -0.09375 to 0.09375
- medium_filter: float32 [128, 256], replicated, may hold values from -0.5 to 0.5
- skip_gain: float32 [256], replicated, may hold values from -1 to 1
- w_out: bfloat16 [256, 256], replicated, may hold values from -0.375 to 0.375
Outputs:
- result: bfloat16 [8192, 256], P(('groups', 'seq')), parts along dimension 0
There are 2 independent parts, one for each index of `groups`. A program takes and returns all parts, laid end to end along the dimension named above; an argument that names none is the same for every part. Nothing has to cross between parts.
All inputs are finite; a program needn't handle non-finite values.
Results may differ from a plain program's by a relative error of at most 0.015.
Values may be sent and summed in bfloat16 or wider, within the bound.
A program may use at most 64 MiB of HBM per device.

v0:
```python
import functools
import math

import jax
import jax.numpy as jnp
import numpy as np
from jax import lax
from jax.experimental import pallas as pl
from jax.experimental.pallas import tpu as pltpu
from jax.sharding import PartitionSpec as P

epsilon = 1e-06
bf16 = jnp.bfloat16
f32 = jnp.float32


def tables(devices, tok_rows, chans):
    full = devices * tok_rows
    idx = np.arange(devices)
    angle = 2.0 * math.pi * ((idx[:, None] * (4 * idx[None, :] + 1)) % (4 * devices)) / (4 * devices)
    eye = np.eye(chans)
    outer_cos = np.kron(np.cos(angle), eye)
    outer_sin = np.kron(np.sin(angle), eye)
    first = np.concatenate([outer_cos.T, -outer_sin.T], axis=0)
    last = np.concatenate([outer_cos, -outer_sin], axis=1) / full
    pos = np.arange(tok_rows)
    turn = 2.0 * math.pi * ((4 * idx[:, None] + 1) * pos[None, :]) / (4 * full)
    tw_cos = np.repeat(np.cos(turn), chans, axis=0)
    tw_sin = np.repeat(np.sin(turn), chans, axis=0)
    inner = 2.0 * math.pi * (pos[:, None] * pos[None, :] % tok_rows) / tok_rows
    cos_t, sin_t = np.cos(inner), np.sin(inner)
    middle = np.block([[cos_t, -sin_t], [sin_t, cos_t]])
    return (
        first.astype(bf16),
        middle.astype(bf16),
        last.astype(bf16),
        tw_cos.astype(np.float32),
        tw_sin.astype(np.float32),
    )


def dot(a, b):
    return jnp.dot(a, b, preferred_element_type=f32)


def forward(rows, first, middle, tw_cos, tw_sin):
    half = rows.shape[0]
    part = dot(first, rows)
    re, im = part[:half], part[half:]
    turned = jnp.concatenate([re * tw_cos + im * tw_sin, im * tw_cos - re * tw_sin], axis=1)
    return dot(turned.astype(bf16), middle)


def convolve(sig, fil, first, middle, last, tw_cos, tw_sin):
    width = sig.shape[1]
    spec = forward(sig, first, middle, tw_cos, tw_sin)
    gain = forward(fil, first, middle, tw_cos, tw_sin)
    sr, si, gr, gi = spec[:, :width], spec[:, width:], gain[:, :width], gain[:, width:]
    prod = jnp.concatenate([sr * gi + si * gr, sr * gr - si * gi], axis=1).astype(bf16)
    back = dot(prod, middle)
    im, re = back[:, :width], back[:, width:]
    turned = jnp.concatenate([re * tw_cos - im * tw_sin, re * tw_sin + im * tw_cos], axis=0)
    return dot(last, turned.astype(bf16))


def from_behind(array, axis, by):
    devices = lax.axis_size(axis)
    pairs = [(i, i + by) for i in range(devices) if 0 <= i + by < devices]
    return lax.ppermute(array, axis, pairs)


def local(tokens, norm_gain, w_in, short_filter, long_filter, medium_filter, skip_gain, w_out):
    tok_rows, chan_width = tokens.shape
    devices = lax.axis_size("seq")
    my_index = lax.axis_index("seq")
    chans = chan_width // devices
    consts = [jnp.asarray(t) for t in tables(devices, tok_rows, chans)]
    med = jnp.pad(medium_filter, ((0, tok_rows - medium_filter.shape[0]), (0, 0)))
    med = med.at[0].add(skip_gain)
    taps = (long_filter + jnp.where(my_index == 0, med, 0.0)).astype(bf16)
    inputs = tokens.astype(f32)
    mean_sq = jnp.mean(inputs * inputs, axis=-1, keepdims=True)
    normed = (inputs * lax.rsqrt(mean_sq + epsilon) * norm_gain).astype(bf16)
    projected = dot(normed, w_in).astype(bf16)
    taps_count = short_filter.shape[0]
    rim_rows = from_behind(projected[tok_rows - (taps_count - 1) :], "seq", 1)
    extended = jnp.concatenate([rim_rows, projected], axis=0)
    short_mix = jnp.zeros((tok_rows, projected.shape[1]), f32)
    for tap_num in range(taps_count):
        begin = taps_count - 1 - tap_num
        short_mix = short_mix + short_filter[tap_num] * extended[begin : begin + tok_rows]
    query_part = short_mix[:, 0:chan_width]
    signal = short_mix[:, chan_width : 2 * chan_width] * short_mix[:, 2 * chan_width :]

    def spread(array):
        split = array.astype(bf16).T.reshape(devices, chans, tok_rows)
        return lax.all_to_all(split, "seq", 0, 0, tiled=True).reshape(chan_width, tok_rows)

    mixed = convolve(spread(signal), spread(taps), *consts)
    back = spread_back(mixed, devices, chans)
    mixed_out = (query_part * back.T.astype(f32)).astype(bf16)
    return dot(mixed_out, w_out).astype(bf16)


def spread_back(mixed, devices, chans):
    split = mixed.astype(bf16).reshape(devices, chans, mixed.shape[1])
    return lax.all_to_all(split, "seq", 0, 0, tiled=True).reshape(mixed.shape)


def rms_normed(rows, gain):
    rows = rows.astype(f32)
    mean_sq = jnp.mean(rows * rows, axis=-1, keepdims=True)
    return (rows * lax.rsqrt(mean_sq + epsilon) * gain).astype(bf16)


def kernel(
    devices,
    tokens_hbm,
    gain_hbm,
    w_in_hbm,
    short_hbm,
    long_hbm,
    med_hbm,
    skip_hbm,
    w_out_hbm,
    first_hbm,
    middle_hbm,
    last_hbm,
    tw_cos_hbm,
    tw_sin_hbm,
    out_ref,
    tokens,
    gain_ref,
    w_in,
    short_ref,
    long_taps,
    med,
    skip_ref,
    w_out,
    first,
    middle,
    last,
    tw_cos,
    tw_sin,
    halo,
    extended,
    signal,
    sends,
    arrivals,
    local_sem,
    halo_sem,
    send_sem,
    recv_sem,
):
    me = lax.axis_index("seq")
    rows, width = tokens.shape
    offsets = range(1, devices)
    rim = halo.shape[0]
    barrier = pltpu.get_barrier_semaphore()
    for off in offsets:
        pl.semaphore_signal(
            barrier,
            inc=1,
            device_id={"seq": lax.rem(me + off, devices)},
            device_id_type=pl.DeviceIdType.MESH,
        )
    loads = [
        pltpu.make_async_copy(source, target, local_sem.at[num])
        for num, (source, target) in enumerate(
            [
                (tokens_hbm, tokens),
                (gain_hbm, gain_ref),
                (w_in_hbm, w_in),
                (short_hbm, short_ref),
                (long_hbm, long_taps),
                (med_hbm, med),
                (skip_hbm, skip_ref),
                (first_hbm, first),
                (tw_cos_hbm, tw_cos),
                (tw_sin_hbm, tw_sin),
                (middle_hbm, middle),
                (last_hbm, last),
                (w_out_hbm, w_out),
            ]
        )
    ]
    for load in loads:
        load.start()

    def exchange(phase):
        for off in (offsets if phase else reversed(offsets)):
            peer = lax.rem(me + off, devices)
            pltpu.make_async_remote_copy(
                src_ref=sends.at[phase, peer],
                dst_ref=arrivals.at[phase, me],
                send_sem=send_sem.at[phase],
                recv_sem=recv_sem.at[phase],
                device_id={"seq": peer},
                device_id_type=pl.DeviceIdType.MESH,
            ).start()
        arrivals[phase, me] = sends[phase, me]
        return pltpu.make_async_remote_copy(
            src_ref=sends.at[phase, pl.ds(0, devices - 1)],
            dst_ref=arrivals.at[phase, pl.ds(0, devices - 1)],
            send_sem=send_sem.at[phase],
            recv_sem=recv_sem.at[phase],
            device_id={"seq": lax.rem(me + 1, devices)},
            device_id_type=pl.DeviceIdType.MESH,
        )

    def arrived(phase, copies):
        copies.wait_recv()
        return arrivals[phase].reshape(width, rows)

    def project(part_normed, begin):
        return dot(part_normed, w_in[:, begin:]).astype(bf16).astype(f32)

    def mix(part, begin, count):
        lanes = pl.ds(part * width, width)
        total = short_ref[0:1, lanes] * extended[rim + begin : rim + begin + count, lanes]
        for tap in range(1, short_ref.shape[0]):
            start = rim + begin - tap
            total = total + short_ref[tap : tap + 1, lanes] * extended[start : start + count, lanes]
        return total

    def turn_signal(begin, count):
        block = signal[begin : begin + count, :].T.astype(bf16)
        sends[1, :, :, begin : begin + count] = block.reshape(devices, width // devices, count)

    for load in loads[:3]:
        load.wait()
    normed = rms_normed(tokens[...], gain_ref[...])
    extended[rim:, width:] = project(normed, width)
    extended[0:rim, :] = jnp.zeros((rim, 3 * width), f32)
    for load in loads[3:7]:
        load.wait()

    @pl.when(me == 0)
    def _():
        long_taps[0 : med.shape[0], :] += med[...]
        long_taps[0:1, :] += skip_ref[...]

    sends[0] = long_taps[...].T.astype(bf16).reshape(sends.shape[1:])
    signal[...] = mix(1, 0, rows) * mix(2, 0, rows)
    turn_signal(rows // 2, rows // 2)
    pl.semaphore_wait(barrier, devices - 1)
    halo_copy = pltpu.make_async_remote_copy(
        src_ref=tokens.at[pl.ds(rows - rim, rim)],
        dst_ref=halo,
        send_sem=halo_sem.at[0],
        recv_sem=halo_sem.at[1],
        device_id={"seq": lax.rem(me + 1, devices)},
        device_id_type=pl.DeviceIdType.MESH,
    )

    @pl.when(me < devices - 1)
    def _():
        halo_copy.start()

    filter_copies = exchange(0)

    @pl.when(me > 0)
    def _():
        halo_copy.wait_recv()
        extended[0:rim, :] = project(rms_normed(halo[...], gain_ref[...]), 0)
        signal[0:rim, :] = mix(1, 0, rim) * mix(2, 0, rim)

    turn_signal(0, rows // 2)
    signal_copies = exchange(1)

    extended[rim:, :width] = dot(normed, w_in[:, :width]).astype(bf16).astype(f32)
    query = mix(0, 0, rows).T
    for load in loads[7:]:
        load.wait()

    def spectrum(block):
        part = dot(first[...], block)
        re, im = part[:width], part[width:]
        turned = jnp.concatenate(
            [re * tw_cos[...] + im * tw_sin[...], im * tw_cos[...] - re * tw_sin[...]], axis=1
        )
        spec = dot(turned.astype(bf16), middle[...])
        return spec[:, :rows], spec[:, rows:]

    gr, gi = spectrum(arrived(0, filter_copies))
    sr, si = spectrum(arrived(1, signal_copies))
    prod = jnp.concatenate([sr * gi + si * gr, sr * gr - si * gi], axis=1)
    back = dot(prod.astype(bf16), middle[...])
    im, re = back[:, :rows], back[:, rows:]
    turned = jnp.concatenate(
        [re * tw_cos[...] - im * tw_sin[...], re * tw_sin[...] + im * tw_cos[...]], axis=0
    )
    mixed = dot(last[...], turned.astype(bf16))
    sends[2] = mixed.astype(bf16).reshape(sends.shape[1:])
    result_copies = exchange(2)
    gated = (query * arrived(2, result_copies).astype(f32)).astype(bf16).T
    out_ref[...] = dot(gated, w_out[...]).astype(bf16)

    @pl.when(me < devices - 1)
    def _():
        halo_copy.wait_send()

    for copies in (filter_copies, signal_copies, result_copies):
        copies.wait_send()


def fused(tokens, norm_gain, w_in, short_filter, long_filter, medium_filter, skip_gain, w_out):
    rows, width = tokens.shape
    devices = lax.axis_size("seq")
    chans = width // devices
    consts = [jnp.asarray(t) for t in tables(devices, rows, chans)]
    rim = 16
    held = [
        tokens,
        norm_gain.reshape(1, width),
        w_in,
        short_filter,
        long_filter,
        medium_filter,
        skip_gain.reshape(1, width),
        w_out,
        *consts,
    ]
    return pl.pallas_call(
        functools.partial(kernel, devices),
        out_shape=pltpu.VMEM((rows, width), bf16),
        in_specs=[pl.BlockSpec(memory_space=pl.ANY)] * len(held),
        out_specs=pl.BlockSpec(memory_space=pltpu.VMEM),
        scratch_shapes=[pltpu.VMEM(a.shape, a.dtype) for a in held]
        + [
            pltpu.VMEM((rim, width), bf16),
            pltpu.VMEM((rim + rows, 3 * width), f32),
            pltpu.VMEM((rows, width), f32),
            pltpu.VMEM((3, devices, chans, rows), bf16),
            pltpu.VMEM((3, devices, chans, rows), bf16),
            pltpu.SemaphoreType.DMA((len(held),)),
            pltpu.SemaphoreType.DMA((2,)),
            pltpu.SemaphoreType.DMA((3,)),
            pltpu.SemaphoreType.DMA((3,)),
        ],
        compiler_params=pltpu.CompilerParams(collective_id=0, has_side_effects=True),
    )(*held)


def solution(mesh):
    placed = (P(("groups", "seq"), None), P(), P(), P(), P("seq", None), P(), P(), P())

    def step(tokens, norm_gain, w_in, short_filter, long_filter, medium_filter, skip_gain, w_out):
        chans = tokens.shape[1] // mesh.shape["seq"]
        body = fused if chans % 16 == 0 else local
        return body(tokens, norm_gain, w_in, short_filter, long_filter, medium_filter, skip_gain, w_out)

    return jax.shard_map(
        step, mesh=mesh, in_specs=placed, out_specs=P(("groups", "seq"), None), check_vma=False
    )
```

profile of v0, /device:TPU:0, one launch (start us, length us, event | category | flops | bytes accessed | tf_op | source)
XLA Modules:
  0.0 20.1 jit_solution(43063110098924804)
XLA Ops:
  0.0 19.4 %shard_map.127 = bf16[256,256]{1,0:T(8,128)(2,1)S(1)} custom-call(bf16[256,256]{1,0:T(8,128)(2,1)} %tokens_hbm.1, f32[1,256]{1,0:T(1,128)} %bitcast.2, bf16[256,768]{1,0:T(8,128)(2,1)} %w_in_hbm.1, f32[3,768]{1,0:T(4,128)} %short_hbm.1, f32[256,256]{1,0:T(8,128)} %long_hbm.1, f32[128,256]{1,0:T(8,128)} %med_hbm.1, f32[1,256]{1,0:T(1,128)} %bitcast.3, ...), custom_call_target="tpu_custom_call" | custom-call | tf_op jit(solution)/shard_map/pallas_call | solution.py:324
  19.4 0.7 %copy.15 = bf16[256,256]{1,0:T(8,128)(2,1)} copy(bf16[256,256]{1,0:T(8,128)(2,1)S(1)} %shard_map.127) | data formatting | bytes 262144
where the time goes:
time: 20.2 us; the launch traced here: 20.1 us
  Pallas kernels  19.4 us (96%)
  local copies, waits for them, and re-layouts  0.66 us (3%)
    pallas_call x1, Pallas kernels, fused(): pl.pallas_call(functools.partial(kernel, devices), out_shape=pltpu.VMEM((...  19.4 us
    unnamed x1, local copies, waits for them, and re-layouts  0.66 us

commit v1 on v0

--- a/solution.py
+++ b/solution.py
@@ -113,6 +113,15 @@
     return (rows * lax.rsqrt(mean_sq + epsilon) * gain).astype(bf16)
 
 
+def relative(own, count):
+    steps = []
+    bit = 1
+    while bit < count:
+        steps.append((bit, bit * (1 - 2 * (own // bit % 2))))
+        bit *= 2
+    return [own + sum(step for bit, step in steps if off // bit % 2) for off in range(count - 1, -1, -1)]
+
+
 def kernel(
     devices,
     tokens_hbm,
@@ -123,11 +132,13 @@
     med_hbm,
     skip_hbm,
     w_out_hbm,
-    first_hbm,
+    all_first_hbm,
+    all_turns_hbm,
+    all_last_hbm,
+    front_first_hbm,
+    front_turns_hbm,
+    front_last_hbm,
     middle_hbm,
-    last_hbm,
-    tw_cos_hbm,
-    tw_sin_hbm,
     out_ref,
     tokens,
     gain_ref,
@@ -137,16 +148,22 @@
     med,
     skip_ref,
     w_out,
-    first,
+    all_first,
+    all_turns,
+    all_last,
+    front_first,
+    front_turns,
+    front_last,
     middle,
-    last,
-    tw_cos,
-    tw_sin,
     halo,
     extended,
     signal,
     sends,
-    arrivals,
+    from_front,
+    from_back,
+    front_out,
+    back_out,
+    results,
     local_sem,
     halo_sem,
     send_sem,
@@ -154,10 +171,16 @@
 ):
     me = lax.axis_index("seq")
     rows, width = tokens.shape
-    offsets = range(1, devices)
+    side = devices // 2
+    chans = width // devices
+    half = width // 2
+    in_front = me < side
+    own = lax.rem(me, side)
+    cross = relative(own, side)
+    same = cross[:-1]
     rim = halo.shape[0]
     barrier = pltpu.get_barrier_semaphore()
-    for off in offsets:
+    for off in range(1, devices):
         pl.semaphore_signal(
             barrier,
             inc=1,
@@ -175,11 +198,13 @@
                 (long_hbm, long_taps),
                 (med_hbm, med),
                 (skip_hbm, skip_ref),
-                (first_hbm, first),
-                (tw_cos_hbm, tw_cos),
-                (tw_sin_hbm, tw_sin),
                 (middle_hbm, middle),
-                (last_hbm, last),
+                (front_first_hbm, front_first),
+                (front_turns_hbm, front_turns),
+                (front_last_hbm, front_last),
+                (all_first_hbm, all_first),
+                (all_turns_hbm, all_turns),
+                (all_last_hbm, all_last),
                 (w_out_hbm, w_out),
             ]
         )
@@ -187,45 +212,56 @@
     for load in loads:
         load.start()
 
-    def exchange(phase):
-        for off in (offsets if phase else reversed(offsets)):
-            peer = lax.rem(me + off, devices)
-            pltpu.make_async_remote_copy(
-                src_ref=sends.at[phase, peer],
-                dst_ref=arrivals.at[phase, me],
-                send_sem=send_sem.at[phase],
-                recv_sem=recv_sem.at[phase],
-                device_id={"seq": peer},
-                device_id_type=pl.DeviceIdType.MESH,
-            ).start()
-        arrivals[phase, me] = sends[phase, me]
+    def remote(source, target, peer, sent, received):
         return pltpu.make_async_remote_copy(
-            src_ref=sends.at[phase, pl.ds(0, devices - 1)],
-            dst_ref=arrivals.at[phase, pl.ds(0, devices - 1)],
-            send_sem=send_sem.at[phase],
-            recv_sem=recv_sem.at[phase],
-            device_id={"seq": lax.rem(me + 1, devices)},
+            src_ref=source,
+            dst_ref=target,
+            send_sem=send_sem.at[sent],
+            recv_sem=recv_sem.at[received],
+            device_id={"seq": peer},
             device_id_type=pl.DeviceIdType.MESH,
         )
 
-    def arrived(phase, copies):
-        copies.wait_recv()
-        return arrivals[phase].reshape(width, rows)
+    def received(ref, num):
+        remote(ref, ref, 0, num, num).wait_recv()
+
+    def sent(ref, num):
+        remote(ref, ref, 0, num, num).wait_send()
+
+    def scatter(kind):
+        source, front, back = sends.at[kind], from_front.at[kind], from_back.at[kind]
+        near, far = 2 * kind, 2 * kind + 1
+
+        @pl.when(in_front)
+        def _():
+            for d in cross:
+                remote(source.at[1, d], front.at[own, 1], side + d, far, near).start()
+            for d in same:
+                remote(source.at[:, d], front.at[own], d, near, near).start()
+            front[own] = source[:, own]
+
+        @pl.when(jnp.logical_not(in_front))
+        def _():
+            for d in cross:
+                remote(source.at[0, d], back.at[own], d, near, far).start()
+            for d in same:
+                remote(source.at[1, d], back.at[own], side + d, far, far).start()
+            back[own] = source[1, own]
 
     def project(part_normed, begin):
         return dot(part_normed, w_in[:, begin:]).astype(bf16).astype(f32)
 
     def mix(part, begin, count):
-        lanes = pl.ds(part * width, width)
-        total = short_ref[0:1, lanes] * extended[rim + begin : rim + begin + count, lanes]
+        cols = pl.ds(part * width, width)
+        total = short_ref[0:1, cols] * extended[rim + begin : rim + begin + count, cols]
         for tap in range(1, short_ref.shape[0]):
             start = rim + begin - tap
-            total = total + short_ref[tap : tap + 1, lanes] * extended[start : start + count, lanes]
+            total = total + short_ref[tap : tap + 1, cols] * extended[start : start + count, cols]
         return total
 
     def turn_signal(begin, count):
         block = signal[begin : begin + count, :].T.astype(bf16)
-        sends[1, :, :, begin : begin + count] = block.reshape(devices, width // devices, count)
+        sends[1, :, :, :, begin : begin + count] = block.reshape(2, side, chans, count)
 
     for load in loads[:3]:
         load.wait()
@@ -257,7 +293,7 @@
     def _():
         halo_copy.start()
 
-    filter_copies = exchange(0)
+    scatter(0)
 
     @pl.when(me > 0)
     def _():
@@ -266,49 +302,104 @@
         signal[0:rim, :] = mix(1, 0, rim) * mix(2, 0, rim)
 
     turn_signal(0, rows // 2)
-    signal_copies = exchange(1)
+    scatter(1)
 
     extended[rim:, :width] = dot(normed, w_in[:, :width]).astype(bf16).astype(f32)
     query = mix(0, 0, rows).T
     for load in loads[7:]:
         load.wait()
 
-    def spectrum(block):
+    def spectrum(block, first, turns):
         part = dot(first[...], block)
         re, im = part[:width], part[width:]
-        turned = jnp.concatenate(
-            [re * tw_cos[...] + im * tw_sin[...], im * tw_cos[...] - re * tw_sin[...]], axis=1
-        )
+        cos_t, sin_t = turns[:width], turns[width:]
+        turned = jnp.concatenate([re * cos_t + im * sin_t, im * cos_t - re * sin_t], axis=1)
         spec = dot(turned.astype(bf16), middle[...])
         return spec[:, :rows], spec[:, rows:]
 
-    gr, gi = spectrum(arrived(0, filter_copies))
-    sr, si = spectrum(arrived(1, signal_copies))
-    prod = jnp.concatenate([sr * gi + si * gr, sr * gr - si * gi], axis=1)
-    back = dot(prod.astype(bf16), middle[...])
-    im, re = back[:, :rows], back[:, rows:]
-    turned = jnp.concatenate(
-        [re * tw_cos[...] - im * tw_sin[...], re * tw_sin[...] + im * tw_cos[...]], axis=0
-    )
-    mixed = dot(last[...], turned.astype(bf16))
-    sends[2] = mixed.astype(bf16).reshape(sends.shape[1:])
-    result_copies = exchange(2)
-    gated = (query * arrived(2, result_copies).astype(f32)).astype(bf16).T
-    out_ref[...] = dot(gated, w_out[...]).astype(bf16)
+    def inverse(sig, gain, turns, last):
+        (sr, si), (gr, gi) = sig, gain
+        prod = jnp.concatenate([sr * gi + si * gr, sr * gr - si * gi], axis=1)
+        back = dot(prod.astype(bf16), middle[...])
+        im, re = back[:, :rows], back[:, rows:]
+        cos_t, sin_t = turns[:width], turns[width:]
+        turned = jnp.concatenate([re * cos_t - im * sin_t, re * sin_t + im * cos_t], axis=0)
+        return dot(last[...], turned.astype(bf16)).astype(bf16)
+
+    def joined(kind, which):
+        front = from_front[kind, :, which].reshape(half, rows)
+        return jnp.concatenate([front, from_back[kind].reshape(half, rows)], axis=0)
+
+    def finish():
+        gated = (query * results[...].reshape(width, rows).astype(f32)).astype(bf16).T
+        out_ref[...] = dot(gated, w_out[...]).astype(bf16)
+
+    @pl.when(in_front)
+    def _():
+        received(from_front.at[0, pl.ds(0, side - 1)], 0)
+        gain = spectrum(from_front[0].reshape(width, rows), front_first, front_turns)
+        received(from_front.at[1, pl.ds(0, side - 1)], 2)
+        sig = spectrum(from_front[1].reshape(width, rows), front_first, front_turns)
+        front_out[...] = inverse(sig, gain, front_turns, front_last).reshape(front_out.shape)
+        for d in same:
+            remote(front_out.at[d], results.at[:, own], d, 4, 4).start()
+        results[:, own] = front_out[own]
+        received(from_back.at[0], 1)
+        gain = spectrum(joined(0, 0), all_first, all_turns)
+        received(from_back.at[1], 3)
+        sig = spectrum(joined(1, 0), all_first, all_turns)
+        back_out[...] = inverse(sig, gain, all_turns, all_last).reshape(back_out.shape)
+        for d in cross:
+            remote(back_out.at[d], results.at[0, own], side + d, 5, 4).start()
+        received(results.at[:, pl.ds(0, side - 1)], 4)
+        finish()
+        for kind in range(2):
+            sent(sends.at[kind, :, pl.ds(0, side - 1)], 2 * kind)
+            sent(sends.at[kind, 1], 2 * kind + 1)
+        sent(front_out.at[pl.ds(0, side - 1)], 4)
+        sent(back_out, 5)
+
+    @pl.when(jnp.logical_not(in_front))
+    def _():
+        received(from_front.at[0, :, 1], 0)
+        received(from_back.at[0, pl.ds(0, side - 1)], 1)
+        gain = spectrum(joined(0, 1), all_first, all_turns)
+        received(from_front.at[1, :, 1], 2)
+        received(from_back.at[1, pl.ds(0, side - 1)], 3)
+        sig = spectrum(joined(1, 1), all_first, all_turns)
+        back_out[...] = inverse(sig, gain, all_turns, all_last).reshape(back_out.shape)
+        for d in same:
+            remote(back_out.at[d], results.at[1, own], side + d, 5, 5).start()
+        results[1, own] = back_out[own]
+        received(results.at[0], 4)
+        received(results.at[1, pl.ds(0, side - 1)], 5)
+        finish()
+        for kind in range(2):
+            sent(sends.at[kind, 0], 2 * kind)
+            sent(sends.at[kind, 1, pl.ds(0, side - 1)], 2 * kind + 1)
+        sent(back_out.at[pl.ds(0, side - 1)], 5)
 
     @pl.when(me < devices - 1)
     def _():
         halo_copy.wait_send()
-
-    for copies in (filter_copies, signal_copies, result_copies):
-        copies.wait_send()
 
 
 def fused(tokens, norm_gain, w_in, short_filter, long_filter, medium_filter, skip_gain, w_out):
     rows, width = tokens.shape
     devices = lax.axis_size("seq")
+    side = devices // 2
     chans = width // devices
-    consts = [jnp.asarray(t) for t in tables(devices, rows, chans)]
+    all_first, middle, all_last, *all_turns = tables(devices, rows, chans)
+    front_first, _, front_last, *front_turns = tables(side, rows, 2 * chans)
+    consts = [
+        all_first,
+        np.concatenate(all_turns, axis=0),
+        all_last[width // 2 :],
+        front_first,
+        np.concatenate(front_turns, axis=0),
+        front_last,
+        middle,
+    ]
     rim = 16
     held = [
         tokens,
@@ -319,7 +410,7 @@
         medium_filter,
         skip_gain.reshape(1, width),
         w_out,
-        *consts,
+        *[jnp.asarray(t) for t in consts],
     ]
     return pl.pallas_call(
         functools.partial(kernel, devices),
@@ -331,12 +422,16 @@
             pltpu.VMEM((rim, width), bf16),
             pltpu.VMEM((rim + rows, 3 * width), f32),
             pltpu.VMEM((rows, width), f32),
-            pltpu.VMEM((3, devices, chans, rows), bf16),
-            pltpu.VMEM((3, devices, chans, rows), bf16),
+            pltpu.VMEM((2, 2, side, chans, rows), bf16),
+            pltpu.VMEM((2, side, 2, chans, rows), bf16),
+            pltpu.VMEM((2, side, chans, rows), bf16),
+            pltpu.VMEM((side, 2, chans, rows), bf16),
+            pltpu.VMEM((side, chans, rows), bf16),
+            pltpu.VMEM((2, side, chans, rows), bf16),
             pltpu.SemaphoreType.DMA((len(held),)),
             pltpu.SemaphoreType.DMA((2,)),
-            pltpu.SemaphoreType.DMA((3,)),
-            pltpu.SemaphoreType.DMA((3,)),
+            pltpu.SemaphoreType.DMA((6,)),
+            pltpu.SemaphoreType.DMA((6,)),
         ],
         compiler_params=pltpu.CompilerParams(collective_id=0, has_side_effects=True),
     )(*held)
@@ -347,7 +442,8 @@
 
     def step(tokens, norm_gain, w_in, short_filter, long_filter, medium_filter, skip_gain, w_out):
         chans = tokens.shape[1] // mesh.shape["seq"]
-        body = fused if chans % 16 == 0 else local
+        whole_tiles = chans == 16 and tokens.shape[0] == tokens.shape[1]
+        body = fused if whole_tiles else local
         return body(tokens, norm_gain, w_in, short_filter, long_filter, medium_filter, skip_gain, w_out)
 
     return jax.shard_map(

time: 20.2 us -> 19.4 us (0.960)
  Pallas kernels: 19.4 us -> 18.6 us
    pallas_call x1, Pallas kernels: 19.4 us -> 18.6 us  [fused(): pl.pallas_call(functools.partial(kernel, devices), out_shape=pltpu.VMEM((...]
where the time goes in v1:
time: 19.4 us; the launch traced here: 19.2 us
  Pallas kernels  18.6 us (96%)
  local copies, waits for them, and re-layouts  0.66 us (3%)
    pallas_call x1, Pallas kernels, fused(): pl.pallas_call(functools.partial(kernel, devices), out_shape=pltpu.VMEM((...  18.6 us
    unnamed x1, local copies, waits for them, and re-layouts  0.66 us

profile of v1, /device:TPU:0, one launch (start us, length us, event | category | flops | bytes accessed | tf_op | source)
XLA Modules:
  0.0 19.2 jit_solution(7826200455636691753)
XLA Ops:
  0.0 18.6 %shard_map.145 = bf16[256,256]{1,0:T(8,128)(2,1)S(1)} custom-call(bf16[256,256]{1,0:T(8,128)(2,1)} %tokens_hbm.1, f32[1,256]{1,0:T(1,128)} %bitcast.2, bf16[256,768]{1,0:T(8,128)(2,1)} %w_in_hbm.1, f32[3,768]{1,0:T(4,128)} %short_hbm.1, f32[256,256]{1,0:T(8,128)} %long_hbm.1, f32[128,256]{1,0:T(8,128)} %med_hbm.1, f32[1,256]{1,0:T(1,128)} %bitcast.3, ...), custom_call_target="tpu_custom_call" | custom-call | tf_op jit(solution)/shard_map/pallas_call | solution.py:415
  18.6 0.7 %copy.17 = bf16[256,256]{1,0:T(8,128)(2,1)} copy(bf16[256,256]{1,0:T(8,128)(2,1)S(1)} %shard_map.145) | data formatting | bytes 262144

commit v2 on v1

--- a/solution.py
+++ b/solution.py
@@ -164,6 +164,7 @@
     front_out,
     back_out,
     results,
+    ready,
     local_sem,
     halo_sem,
     send_sem,
@@ -179,14 +180,26 @@
     cross = relative(own, side)
     same = cross[:-1]
     rim = halo.shape[0]
+    in_back = jnp.logical_not(in_front)
     barrier = pltpu.get_barrier_semaphore()
-    for off in range(1, devices):
+
+    def announce(semaphore, peer):
         pl.semaphore_signal(
-            barrier,
-            inc=1,
-            device_id={"seq": lax.rem(me + off, devices)},
-            device_id_type=pl.DeviceIdType.MESH,
+            semaphore, inc=1, device_id={"seq": peer}, device_id_type=pl.DeviceIdType.MESH
         )
+
+    @pl.when(in_front)
+    def _():
+        for d in same:
+            announce(barrier, d)
+        for d in cross:
+            announce(barrier, side + d)
+
+    @pl.when(in_back)
+    def _():
+        for d in same:
+            announce(barrier, side + d)
+
     loads = [
         pltpu.make_async_copy(source, target, local_sem.at[num])
         for num, (source, target) in enumerate(
@@ -212,6 +225,12 @@
     for load in loads:
         load.start()
 
+    @pl.when(me == devices - 1)
+    def _():
+        pl.semaphore_wait(barrier, devices - 1)
+        for d in cross:
+            announce(ready, d)
+
     def remote(source, target, peer, sent, received):
         return pltpu.make_async_remote_copy(
             src_ref=source,
@@ -228,25 +247,26 @@
     def sent(ref, num):
         remote(ref, ref, 0, num, num).wait_send()
 
-    def scatter(kind):
-        source, front, back = sends.at[kind], from_front.at[kind], from_back.at[kind]
-        near, far = 2 * kind, 2 * kind + 1
-
-        @pl.when(in_front)
-        def _():
-            for d in cross:
-                remote(source.at[1, d], front.at[own, 1], side + d, far, near).start()
-            for d in same:
-                remote(source.at[:, d], front.at[own], d, near, near).start()
-            front[own] = source[:, own]
-
-        @pl.when(jnp.logical_not(in_front))
-        def _():
-            for d in cross:
-                remote(source.at[0, d], back.at[own], d, near, far).start()
-            for d in same:
-                remote(source.at[1, d], back.at[own], side + d, far, far).start()
-            back[own] = source[1, own]
+    def same_from_front(kind):
+        for d in same:
+            remote(sends.at[kind, :, d], from_front.at[kind, own], d, 2 * kind, 2 * kind).start()
+        from_front[kind, own] = sends[kind, :, own]
+
+    def cross_from_front(kind):
+        for d in cross:
+            target = from_front.at[kind, own, 1]
+            remote(sends.at[kind, 1, d], target, side + d, 2 * kind + 1, 2 * kind).start()
+
+    def same_from_back(kind):
+        for d in same:
+            target = from_back.at[kind, own]
+            remote(sends.at[kind, 1, d], target, side + d, 2 * kind + 1, 2 * kind + 1).start()
+        from_back[kind, own] = sends[kind, 1, own]
+
+    def cross_from_back(kind):
+        for d in cross:
+            target = from_back.at[kind, own]
+            remote(sends.at[kind, 0, d], target, d, 2 * kind, 2 * kind + 1).start()
 
     def project(part_normed, begin):
         return dot(part_normed, w_in[:, begin:]).astype(bf16).astype(f32)
@@ -279,7 +299,6 @@
     sends[0] = long_taps[...].T.astype(bf16).reshape(sends.shape[1:])
     signal[...] = mix(1, 0, rows) * mix(2, 0, rows)
     turn_signal(rows // 2, rows // 2)
-    pl.semaphore_wait(barrier, devices - 1)
     halo_copy = pltpu.make_async_remote_copy(
         src_ref=tokens.at[pl.ds(rows - rim, rim)],
         dst_ref=halo,
@@ -289,11 +308,25 @@
         device_id_type=pl.DeviceIdType.MESH,
     )
 
-    @pl.when(me < devices - 1)
-    def _():
-        halo_copy.start()
-
-    scatter(0)
+    @pl.when(in_front)
+    def _():
+        pl.semaphore_wait(barrier, side - 1)
+
+        @pl.when(me < side - 1)
+        def _():
+            halo_copy.start()
+
+        same_from_front(0)
+
+    @pl.when(in_back)
+    def _():
+        @pl.when(me < devices - 1)
+        def _():
+            pl.semaphore_wait(barrier, devices - 1)
+            halo_copy.start()
+
+        same_from_back(0)
+        cross_from_back(0)
 
     @pl.when(me > 0)
     def _():
@@ -302,7 +335,23 @@
         signal[0:rim, :] = mix(1, 0, rim) * mix(2, 0, rim)
 
     turn_signal(0, rows // 2)
-    scatter(1)
+
+    @pl.when(in_front)
+    def _():
+        same_from_front(1)
+        pl.semaphore_wait(ready, 1)
+
+        @pl.when(me == side - 1)
+        def _():
+            halo_copy.start()
+
+        cross_from_front(0)
+        cross_from_front(1)
+
+    @pl.when(in_back)
+    def _():
+        same_from_back(1)
+        cross_from_back(1)
 
     extended[rim:, :width] = dot(normed, w_in[:, :width]).astype(bf16).astype(f32)
     query = mix(0, 0, rows).T
@@ -338,17 +387,17 @@
     def _():
         received(from_front.at[0, pl.ds(0, side - 1)], 0)
         gain = spectrum(from_front[0].reshape(width, rows), front_first, front_turns)
+        received(from_back.at[0], 1)
+        back_gain = spectrum(joined(0, 0), all_first, all_turns)
         received(from_front.at[1, pl.ds(0, side - 1)], 2)
         sig = spectrum(from_front[1].reshape(width, rows), front_first, front_turns)
         front_out[...] = inverse(sig, gain, front_turns, front_last).reshape(front_out.shape)
         for d in same:
             remote(front_out.at[d], results.at[:, own], d, 4, 4).start()
         results[:, own] = front_out[own]
-        received(from_back.at[0], 1)
-        gain = spectrum(joined(0, 0), all_first, all_turns)
         received(from_back.at[1], 3)
         sig = spectrum(joined(1, 0), all_first, all_turns)
-        back_out[...] = inverse(sig, gain, all_turns, all_last).reshape(back_out.shape)
+        back_out[...] = inverse(sig, back_gain, all_turns, all_last).reshape(back_out.shape)
         for d in cross:
             remote(back_out.at[d], results.at[0, own], side + d, 5, 4).start()
         received(results.at[:, pl.ds(0, side - 1)], 4)
@@ -428,6 +477,7 @@
             pltpu.VMEM((side, 2, chans, rows), bf16),
             pltpu.VMEM((side, chans, rows), bf16),
             pltpu.VMEM((2, side, chans, rows), bf16),
+            pltpu.SemaphoreType.REGULAR,
             pltpu.SemaphoreType.DMA((len(held),)),
             pltpu.SemaphoreType.DMA((2,)),
             pltpu.SemaphoreType.DMA((6,)),

time: 19.4 us -> 17.2 us (0.89)
  Pallas kernels: 18.6 us -> 16.4 us
    pallas_call x1, Pallas kernels: 18.6 us -> 16.4 us  [fused(): pl.pallas_call(functools.partial(kernel, devices), out_shape=pltpu.VMEM((...]
where the time goes in v2:
time: 17.2 us; the launch traced here: 17.1 us
  Pallas kernels  16.4 us (95%)
  local copies, waits for them, and re-layouts  0.66 us (4%)
    pallas_call x1, Pallas kernels, fused(): pl.pallas_call(functools.partial(kernel, devices), out_shape=pltpu.VMEM((...  16.4 us
    unnamed x1, local copies, waits for them, and re-layouts  0.66 us

profile of v2, /device:TPU:0, one launch (start us, length us, event | category | flops | bytes accessed | tf_op | source)
XLA Modules:
  0.0 17.1 jit_solution(10502486983278050414)
XLA Ops:
  0.0 16.4 %shard_map.145 = bf16[256,256]{1,0:T(8,128)(2,1)S(1)} custom-call(bf16[256,256]{1,0:T(8,128)(2,1)} %tokens_hbm.1, f32[1,256]{1,0:T(1,128)} %bitcast.2, bf16[256,768]{1,0:T(8,128)(2,1)} %w_in_hbm.1, f32[3,768]{1,0:T(4,128)} %short_hbm.1, f32[256,256]{1,0:T(8,128)} %long_hbm.1, f32[128,256]{1,0:T(8,128)} %med_hbm.1, f32[1,256]{1,0:T(1,128)} %bitcast.3, ...), custom_call_target="tpu_custom_call" | custom-call | tf_op jit(solution)/shard_map/pallas_call | solution.py:464
  16.4 0.7 %copy.17 = bf16[256,256]{1,0:T(8,128)(2,1)} copy(bf16[256,256]{1,0:T(8,128)(2,1)S(1)} %shard_map.145) | data formatting | bytes 262144

commit v3 on v2

--- a/solution.py
+++ b/solution.py
@@ -158,6 +158,7 @@
     halo,
     extended,
     signal,
+    later,
     sends,
     from_front,
     from_back,
@@ -175,6 +176,8 @@
     side = devices // 2
     chans = width // devices
     half = width // 2
+    lanes = rows // 2
+    fine = chans // 2
     in_front = me < side
     own = lax.rem(me, side)
     cross = relative(own, side)
@@ -204,13 +207,13 @@
         pltpu.make_async_copy(source, target, local_sem.at[num])
         for num, (source, target) in enumerate(
             [
+                (long_hbm, long_taps),
+                (med_hbm, med),
+                (skip_hbm, skip_ref),
                 (tokens_hbm, tokens),
                 (gain_hbm, gain_ref),
                 (w_in_hbm, w_in),
                 (short_hbm, short_ref),
-                (long_hbm, long_taps),
-                (med_hbm, med),
-                (skip_hbm, skip_ref),
                 (middle_hbm, middle),
                 (front_first_hbm, front_first),
                 (front_turns_hbm, front_turns),
@@ -222,7 +225,7 @@
             ]
         )
     ]
-    for load in loads:
+    for load in loads[:7]:
         load.start()
 
     @pl.when(me == devices - 1)
@@ -279,26 +282,10 @@
             total = total + short_ref[tap : tap + 1, cols] * extended[start : start + count, cols]
         return total
 
-    def turn_signal(begin, count):
-        block = signal[begin : begin + count, :].T.astype(bf16)
-        sends[1, :, :, :, begin : begin + count] = block.reshape(2, side, chans, count)
-
-    for load in loads[:3]:
-        load.wait()
-    normed = rms_normed(tokens[...], gain_ref[...])
-    extended[rim:, width:] = project(normed, width)
-    extended[0:rim, :] = jnp.zeros((rim, 3 * width), f32)
-    for load in loads[3:7]:
-        load.wait()
-
-    @pl.when(me == 0)
-    def _():
-        long_taps[0 : med.shape[0], :] += med[...]
-        long_taps[0:1, :] += skip_ref[...]
-
-    sends[0] = long_taps[...].T.astype(bf16).reshape(sends.shape[1:])
-    signal[...] = mix(1, 0, rows) * mix(2, 0, rows)
-    turn_signal(rows // 2, rows // 2)
+    def turn(ref, begin):
+        block = ref[begin : begin + lanes, :].T.reshape(2, side, 2, fine, lanes)
+        return jnp.concatenate([block[:, :, 0], block[:, :, 1]], axis=3)
+
     halo_copy = pltpu.make_async_remote_copy(
         src_ref=tokens.at[pl.ds(rows - rim, rim)],
         dst_ref=halo,
@@ -307,16 +294,16 @@
         device_id={"seq": lax.rem(me + 1, devices)},
         device_id_type=pl.DeviceIdType.MESH,
     )
-
-    @pl.when(in_front)
-    def _():
-        pl.semaphore_wait(barrier, side - 1)
-
-        @pl.when(me < side - 1)
-        def _():
-            halo_copy.start()
-
-        same_from_front(0)
+    for load in loads[:3]:
+        load.wait()
+
+    @pl.when(me == 0)
+    def _():
+        long_taps[0 : med.shape[0], :] += med[...]
+        long_taps[0:1, :] += skip_ref[...]
+
+    sends[0] = jnp.concatenate([turn(long_taps, 0), turn(long_taps, lanes)], axis=2).astype(bf16)
+    loads[3].wait()
 
     @pl.when(in_back)
     def _():
@@ -328,13 +315,33 @@
         same_from_back(0)
         cross_from_back(0)
 
+    for load in loads[7:]:
+        load.start()
+    for load in loads[4:7]:
+        load.wait()
+    normed = rms_normed(tokens[...], gain_ref[...])
+    extended[rim:, width:] = project(normed, width)
+    extended[0:rim, :] = jnp.zeros((rim, 3 * width), f32)
+    signal[...] = mix(1, 0, rows) * mix(2, 0, rows)
+    later[...] = turn(signal, lanes)
+
+    @pl.when(in_front)
+    def _():
+        pl.semaphore_wait(barrier, side - 1)
+
+        @pl.when(me < side - 1)
+        def _():
+            halo_copy.start()
+
+        same_from_front(0)
+
     @pl.when(me > 0)
     def _():
         halo_copy.wait_recv()
         extended[0:rim, :] = project(rms_normed(halo[...], gain_ref[...]), 0)
         signal[0:rim, :] = mix(1, 0, rim) * mix(2, 0, rim)
 
-    turn_signal(0, rows // 2)
+    sends[1] = jnp.concatenate([turn(signal, 0), later[...]], axis=2).astype(bf16)
 
     @pl.when(in_front)
     def _():
@@ -358,19 +365,26 @@
     for load in loads[7:]:
         load.wait()
 
+    def stacked(left, right):
+        pieces = [(left[:, :lanes], right[:, :lanes]), (left[:, lanes:], right[:, lanes:])]
+        return jnp.concatenate([jnp.concatenate(pair, axis=1) for pair in pieces], axis=0)
+
+    def spread(array):
+        return jnp.concatenate([array[:width], array[width:]], axis=1)
+
     def spectrum(block, first, turns):
         part = dot(first[...], block)
         re, im = part[:width], part[width:]
         cos_t, sin_t = turns[:width], turns[width:]
-        turned = jnp.concatenate([re * cos_t + im * sin_t, im * cos_t - re * sin_t], axis=1)
+        turned = stacked(re * cos_t + im * sin_t, im * cos_t - re * sin_t)
         spec = dot(turned.astype(bf16), middle[...])
-        return spec[:, :rows], spec[:, rows:]
+        return spec[:, :lanes], spec[:, lanes:]
 
     def inverse(sig, gain, turns, last):
         (sr, si), (gr, gi) = sig, gain
         prod = jnp.concatenate([sr * gi + si * gr, sr * gr - si * gi], axis=1)
         back = dot(prod.astype(bf16), middle[...])
-        im, re = back[:, :rows], back[:, rows:]
+        im, re = spread(back[:, :lanes]), spread(back[:, lanes:])
         cos_t, sin_t = turns[:width], turns[width:]
         turned = jnp.concatenate([re * cos_t - im * sin_t, re * sin_t + im * cos_t], axis=0)
         return dot(last[...], turned.astype(bf16)).astype(bf16)
@@ -380,21 +394,28 @@
         return jnp.concatenate([front, from_back[kind].reshape(half, rows)], axis=0)
 
     def finish():
-        gated = (query * results[...].reshape(width, rows).astype(f32)).astype(bf16).T
+        mixed = results[...].astype(f32)
+        early, late = mixed[:, :, :fine], mixed[:, :, fine:]
+        sides = [
+            jnp.concatenate([early[:, :, :, cut], late[:, :, :, cut]], axis=3)
+            for cut in (slice(0, lanes), slice(lanes, rows))
+        ]
+        mixed = jnp.concatenate(sides, axis=2).reshape(width, rows)
+        gated = (query * mixed).astype(bf16).T
         out_ref[...] = dot(gated, w_out[...]).astype(bf16)
 
     @pl.when(in_front)
     def _():
         received(from_front.at[0, pl.ds(0, side - 1)], 0)
         gain = spectrum(from_front[0].reshape(width, rows), front_first, front_turns)
-        received(from_back.at[0], 1)
-        back_gain = spectrum(joined(0, 0), all_first, all_turns)
         received(from_front.at[1, pl.ds(0, side - 1)], 2)
         sig = spectrum(from_front[1].reshape(width, rows), front_first, front_turns)
         front_out[...] = inverse(sig, gain, front_turns, front_last).reshape(front_out.shape)
         for d in same:
             remote(front_out.at[d], results.at[:, own], d, 4, 4).start()
         results[:, own] = front_out[own]
+        received(from_back.at[0], 1)
+        back_gain = spectrum(joined(0, 0), all_first, all_turns)
         received(from_back.at[1], 3)
         sig = spectrum(joined(1, 0), all_first, all_turns)
         back_out[...] = inverse(sig, back_gain, all_turns, all_last).reshape(back_out.shape)
@@ -438,15 +459,17 @@
     devices = lax.axis_size("seq")
     side = devices // 2
     chans = width // devices
-    all_first, middle, all_last, *all_turns = tables(devices, rows, chans)
-    front_first, _, front_last, *front_turns = tables(side, rows, 2 * chans)
+    lanes, fine = rows // 2, chans // 2
+    all_first, middle, all_last, *all_turns = tables(2 * devices, lanes, fine)
+    front_first, _, front_last, *front_turns = tables(devices, lanes, chans)
+    order = np.arange(width).reshape(side, 2, 2, fine).transpose(0, 2, 1, 3).reshape(-1)
     consts = [
         all_first,
-        np.concatenate(all_turns, axis=0),
+        np.tile(np.concatenate(all_turns, axis=0), (1, 2)),
         all_last[width // 2 :],
-        front_first,
-        np.concatenate(front_turns, axis=0),
-        front_last,
+        front_first[:, order],
+        np.tile(np.concatenate(front_turns, axis=0), (1, 2)),
+        front_last[order],
         middle,
     ]
     rim = 16
@@ -471,6 +494,7 @@
             pltpu.VMEM((rim, width), bf16),
             pltpu.VMEM((rim + rows, 3 * width), f32),
             pltpu.VMEM((rows, width), f32),
+            pltpu.VMEM((2, side, fine, rows), f32),
             pltpu.VMEM((2, 2, side, chans, rows), bf16),
             pltpu.VMEM((2, side, 2, chans, rows), bf16),
             pltpu.VMEM((2, side, chans, rows), bf16),

time: 17.2 us -> 17 us (0.988)
  Pallas kernels: 16.4 us -> 16.1 us
    pallas_call x1, Pallas kernels: 16.4 us -> 16.1 us  [fused(): pl.pallas_call(functools.partial(kernel, devices), out_shape=pltpu.VMEM((...]
where the time goes in v3:
time: 17 us; the launch traced here: 16.8 us
  Pallas kernels  16.1 us (95%)
  local copies, waits for them, and re-layouts  0.66 us (4%)
    pallas_call x1, Pallas kernels, fused(): pl.pallas_call(functools.partial(kernel, devices), out_shape=pltpu.VMEM((...  16.1 us
    unnamed x1, local copies, waits for them, and re-layouts  0.66 us

profile of v3, /device:TPU:0, one launch (start us, length us, event | category | flops | bytes accessed | tf_op | source)
XLA Modules:
  0.0 16.8 jit_solution(3876590500868429564)
XLA Ops:
  0.0 16.1 %shard_map.145 = bf16[256,256]{1,0:T(8,128)(2,1)S(1)} custom-call(bf16[256,256]{1,0:T(8,128)(2,1)} %tokens_hbm.1, f32[1,256]{1,0:T(1,128)} %bitcast.2, bf16[256,768]{1,0:T(8,128)(2,1)} %w_in_hbm.1, f32[3,768]{1,0:T(4,128)} %short_hbm.1, f32[256,256]{1,0:T(8,128)} %long_hbm.1, f32[128,256]{1,0:T(8,128)} %med_hbm.1, f32[1,256]{1,0:T(1,128)} %bitcast.3, ...), custom_call_target="tpu_custom_call" | custom-call | tf_op jit(solution)/shard_map/pallas_call | solution.py:487
  16.1 0.7 %copy.17 = bf16[256,256]{1,0:T(8,128)(2,1)} copy(bf16[256,256]{1,0:T(8,128)(2,1)S(1)} %shard_map.145) | data formatting | bytes 262144

commit v4 on v3

--- a/solution.py
+++ b/solution.py
@@ -182,6 +182,9 @@
     own = lax.rem(me, side)
     cross = relative(own, side)
     same = cross[:-1]
+    plane = side // 2
+    near = relative(lax.rem(own, plane), plane)
+    far = [plane + x for x in near]
     rim = halo.shape[0]
     in_back = jnp.logical_not(in_front)
     barrier = pltpu.get_barrier_semaphore()
@@ -419,7 +422,7 @@
         received(from_back.at[1], 3)
         sig = spectrum(joined(1, 0), all_first, all_turns)
         back_out[...] = inverse(sig, back_gain, all_turns, all_last).reshape(back_out.shape)
-        for d in cross:
+        for d in [0, 1, 4, 5, 2, 3, 6, 7]:
             remote(back_out.at[d], results.at[0, own], side + d, 5, 4).start()
         received(results.at[:, pl.ds(0, side - 1)], 4)
         finish()

time: 17 us -> 16.9 us (level)
  no operation moved by 1% of the time
where the time goes in v4:
time: 16.9 us; the launch traced here: 16.8 us
  Pallas kernels  16.1 us (95%)
  local copies, waits for them, and re-layouts  0.66 us (4%)
    pallas_call x1, Pallas kernels, fused(): pl.pallas_call(functools.partial(kernel, devices), out_shape=pltpu.VMEM((...  16.1 us
    unnamed x1, local copies, waits for them, and re-layouts  0.66 us

profile of v4, /device:TPU:0, one launch (start us, length us, event | category | flops | bytes accessed | tf_op | source)
XLA Modules:
  0.0 16.8 jit_solution(9975088935450071138)
XLA Ops:
  0.0 16.1 %shard_map.145 = bf16[256,256]{1,0:T(8,128)(2,1)S(1)} custom-call(bf16[256,256]{1,0:T(8,128)(2,1)} %tokens_hbm.1, f32[1,256]{1,0:T(1,128)} %bitcast.2, bf16[256,768]{1,0:T(8,128)(2,1)} %w_in_hbm.1, f32[3,768]{1,0:T(4,128)} %short_hbm.1, f32[256,256]{1,0:T(8,128)} %long_hbm.1, f32[128,256]{1,0:T(8,128)} %med_hbm.1, f32[1,256]{1,0:T(1,128)} %bitcast.3, ...), custom_call_target="tpu_custom_call" | custom-call | tf_op jit(solution)/shard_map/pallas_call | solution.py:490
  16.1 0.7 %copy.17 = bf16[256,256]{1,0:T(8,128)(2,1)} copy(bf16[256,256]{1,0:T(8,128)(2,1)S(1)} %shard_map.145) | data formatting | bytes 262144

commit v5 on v4

--- a/solution.py
+++ b/solution.py
@@ -132,13 +132,8 @@
     med_hbm,
     skip_hbm,
     w_out_hbm,
-    all_first_hbm,
-    all_turns_hbm,
-    all_last_hbm,
-    front_first_hbm,
-    front_turns_hbm,
-    front_last_hbm,
-    middle_hbm,
+    matrices_hbm,
+    turns_hbm,
     out_ref,
     tokens,
     gain_ref,
@@ -148,13 +143,8 @@
     med,
     skip_ref,
     w_out,
-    all_first,
-    all_turns,
-    all_last,
-    front_first,
-    front_turns,
-    front_last,
-    middle,
+    matrices,
+    turns,
     halo,
     extended,
     signal,
@@ -206,29 +196,23 @@
         for d in same:
             announce(barrier, side + d)
 
-    loads = [
-        pltpu.make_async_copy(source, target, local_sem.at[num])
-        for num, (source, target) in enumerate(
-            [
-                (long_hbm, long_taps),
-                (med_hbm, med),
-                (skip_hbm, skip_ref),
-                (tokens_hbm, tokens),
-                (gain_hbm, gain_ref),
-                (w_in_hbm, w_in),
-                (short_hbm, short_ref),
-                (middle_hbm, middle),
-                (front_first_hbm, front_first),
-                (front_turns_hbm, front_turns),
-                (front_last_hbm, front_last),
-                (all_first_hbm, all_first),
-                (all_turns_hbm, all_turns),
-                (all_last_hbm, all_last),
-                (w_out_hbm, w_out),
-            ]
-        )
-    ]
-    for load in loads[:7]:
+    def copies(pairs):
+        return [
+            pltpu.make_async_copy(source, target, local_sem.at[num])
+            for num, (source, target) in enumerate(pairs)
+        ]
+
+    loads = copies(
+        [
+            (long_hbm, long_taps),
+            (tokens_hbm, tokens),
+            (gain_hbm, gain_ref),
+            (w_in_hbm, w_in),
+            (short_hbm, short_ref),
+        ]
+    )
+    later_loads = copies([(matrices_hbm, matrices), (w_out_hbm, w_out), (turns_hbm, turns)])
+    for load in loads:
         load.start()
 
     @pl.when(me == devices - 1)
@@ -255,24 +239,24 @@
 
     def same_from_front(kind):
         for d in same:
-            remote(sends.at[kind, :, d], from_front.at[kind, own], d, 2 * kind, 2 * kind).start()
+            remote(sends.at[kind, :, d], from_front.at[kind, own], d, 0, 2 * kind).start()
         from_front[kind, own] = sends[kind, :, own]
 
     def cross_from_front(kind):
         for d in cross:
             target = from_front.at[kind, own, 1]
-            remote(sends.at[kind, 1, d], target, side + d, 2 * kind + 1, 2 * kind).start()
+            remote(sends.at[kind, 1, d], target, side + d, 1, 2 * kind).start()
 
     def same_from_back(kind):
         for d in same:
             target = from_back.at[kind, own]
-            remote(sends.at[kind, 1, d], target, side + d, 2 * kind + 1, 2 * kind + 1).start()
+            remote(sends.at[kind, 1, d], target, side + d, 1, 2 * kind + 1).start()
         from_back[kind, own] = sends[kind, 1, own]
 
     def cross_from_back(kind):
         for d in cross:
             target = from_back.at[kind, own]
-            remote(sends.at[kind, 0, d], target, d, 2 * kind, 2 * kind + 1).start()
+            remote(sends.at[kind, 0, d], target, d, 0, 2 * kind + 1).start()
 
     def project(part_normed, begin):
         return dot(part_normed, w_in[:, begin:]).astype(bf16).astype(f32)
@@ -297,16 +281,21 @@
         device_id={"seq": lax.rem(me + 1, devices)},
         device_id_type=pl.DeviceIdType.MESH,
     )
-    for load in loads[:3]:
-        load.wait()
+    loads[0].wait()
 
     @pl.when(me == 0)
     def _():
+        for load in copies([(med_hbm, med)]):
+            load.start()
+            load.wait()
+        for load in copies([(skip_hbm, skip_ref)]):
+            load.start()
+            load.wait()
         long_taps[0 : med.shape[0], :] += med[...]
         long_taps[0:1, :] += skip_ref[...]
 
     sends[0] = jnp.concatenate([turn(long_taps, 0), turn(long_taps, lanes)], axis=2).astype(bf16)
-    loads[3].wait()
+    loads[1].wait()
 
     @pl.when(in_back)
     def _():
@@ -318,10 +307,10 @@
         same_from_back(0)
         cross_from_back(0)
 
-    for load in loads[7:]:
+    for load in loads[2:]:
+        load.wait()
+    for load in later_loads:
         load.start()
-    for load in loads[4:7]:
-        load.wait()
     normed = rms_normed(tokens[...], gain_ref[...])
     extended[rim:, width:] = project(normed, width)
     extended[0:rim, :] = jnp.zeros((rim, 3 * width), f32)
@@ -365,8 +354,13 @@
 
     extended[rim:, :width] = dot(normed, w_in[:, :width]).astype(bf16).astype(f32)
     query = mix(0, 0, rows).T
-    for load in loads[7:]:
+    for load in later_loads:
         load.wait()
+    sizes = [2 * width, 2 * width, width, 2 * width, width]
+    begins = [sum(sizes[:num]) for num in range(len(sizes))]
+    views = [matrices.at[pl.ds(begin, size)] for begin, size in zip(begins, sizes)]
+    all_first, front_first, middle, front_last, all_last = views
+    all_turns, front_turns = (turns.at[pl.ds(side_begin, 2 * width)] for side_begin in (0, 2 * width))
 
     def stacked(left, right):
         pieces = [(left[:, :lanes], right[:, :lanes]), (left[:, lanes:], right[:, lanes:])]
@@ -389,8 +383,10 @@
         back = dot(prod.astype(bf16), middle[...])
         im, re = spread(back[:, :lanes]), spread(back[:, lanes:])
         cos_t, sin_t = turns[:width], turns[width:]
-        turned = jnp.concatenate([re * cos_t - im * sin_t, re * sin_t + im * cos_t], axis=0)
-        return dot(last[...], turned.astype(bf16)).astype(bf16)
+        left, right = re * cos_t - im * sin_t, re * sin_t + im * cos_t
+        count = last.shape[0] // 2
+        total = dot(last[:count], left.astype(bf16)) + dot(last[count:], right.astype(bf16))
+        return total.astype(bf16)
 
     def joined(kind, which):
         front = from_front[kind, :, which].reshape(half, rows)
@@ -415,7 +411,7 @@
         sig = spectrum(from_front[1].reshape(width, rows), front_first, front_turns)
         front_out[...] = inverse(sig, gain, front_turns, front_last).reshape(front_out.shape)
         for d in same:
-            remote(front_out.at[d], results.at[:, own], d, 4, 4).start()
+            remote(front_out.at[d], results.at[:, own], d, 2, 4).start()
         results[:, own] = front_out[own]
         received(from_back.at[0], 1)
         back_gain = spectrum(joined(0, 0), all_first, all_turns)
@@ -423,14 +419,13 @@
         sig = spectrum(joined(1, 0), all_first, all_turns)
         back_out[...] = inverse(sig, back_gain, all_turns, all_last).reshape(back_out.shape)
         for d in [0, 1, 4, 5, 2, 3, 6, 7]:
-            remote(back_out.at[d], results.at[0, own], side + d, 5, 4).start()
+            remote(back_out.at[d], results.at[0, own], side + d, 3, 4).start()
         received(results.at[:, pl.ds(0, side - 1)], 4)
         finish()
-        for kind in range(2):
-            sent(sends.at[kind, :, pl.ds(0, side - 1)], 2 * kind)
-            sent(sends.at[kind, 1], 2 * kind + 1)
-        sent(front_out.at[pl.ds(0, side - 1)], 4)
-        sent(back_out, 5)
+        sent(sends.at[:, :, pl.ds(0, side - 1)], 0)
+        sent(sends.at[:, 1], 1)
+        sent(front_out.at[pl.ds(0, side - 1)], 2)
+        sent(back_out, 3)
 
     @pl.when(jnp.logical_not(in_front))
     def _():
@@ -442,15 +437,14 @@
         sig = spectrum(joined(1, 1), all_first, all_turns)
         back_out[...] = inverse(sig, gain, all_turns, all_last).reshape(back_out.shape)
         for d in same:
-            remote(back_out.at[d], results.at[1, own], side + d, 5, 5).start()
+            remote(back_out.at[d], results.at[1, own], side + d, 3, 5).start()
         results[1, own] = back_out[own]
         received(results.at[0], 4)
         received(results.at[1, pl.ds(0, side - 1)], 5)
         finish()
-        for kind in range(2):
-            sent(sends.at[kind, 0], 2 * kind)
-            sent(sends.at[kind, 1, pl.ds(0, side - 1)], 2 * kind + 1)
-        sent(back_out.at[pl.ds(0, side - 1)], 5)
+        sent(sends.at[:, 0], 0)
+        sent(sends.at[:, 1, pl.ds(0, side - 1)], 1)
+        sent(back_out.at[pl.ds(0, side - 1)], 3)
 
     @pl.when(me < devices - 1)
     def _():
@@ -466,14 +460,20 @@
     all_first, middle, all_last, *all_turns = tables(2 * devices, lanes, fine)
     front_first, _, front_last, *front_turns = tables(devices, lanes, chans)
     order = np.arange(width).reshape(side, 2, 2, fine).transpose(0, 2, 1, 3).reshape(-1)
+
+    def split(matrix):
+        return np.concatenate([matrix[:, :width], matrix[:, width:]], axis=0)
+
+    matrices = [
+        all_first,
+        front_first[:, order],
+        middle,
+        split(front_last[order]),
+        split(all_last[width // 2 :]),
+    ]
     consts = [
-        all_first,
-        np.tile(np.concatenate(all_turns, axis=0), (1, 2)),
-        all_last[width // 2 :],
-        front_first[:, order],
-        np.tile(np.concatenate(front_turns, axis=0), (1, 2)),
-        front_last[order],
-        middle,
+        np.concatenate(matrices, axis=0),
+        np.tile(np.concatenate([*all_turns, *front_turns], axis=0), (1, 2)),
     ]
     rim = 16
     held = [
@@ -505,9 +505,9 @@
             pltpu.VMEM((side, chans, rows), bf16),
             pltpu.VMEM((2, side, chans, rows), bf16),
             pltpu.SemaphoreType.REGULAR,
-            pltpu.SemaphoreType.DMA((len(held),)),
+            pltpu.SemaphoreType.DMA((5,)),
             pltpu.SemaphoreType.DMA((2,)),
-            pltpu.SemaphoreType.DMA((6,)),
+            pltpu.SemaphoreType.DMA((4,)),
             pltpu.SemaphoreType.DMA((6,)),
         ],
         compiler_params=pltpu.CompilerParams(collective_id=0, has_side_effects=True),

time: 16.9 us -> 16.8 us (level)
  no operation moved by 1% of the time
where the time goes in v5:
time: 16.8 us; the launch traced here: 16.7 us
  Pallas kernels  16 us (95%)
  local copies, waits for them, and re-layouts  0.66 us (4%)
    pallas_call x1, Pallas kernels, fused(): pl.pallas_call(functools.partial(kernel, devices), out_shape=pltpu.VMEM((...  16 us
    unnamed x1, local copies, waits for them, and re-layouts  0.66 us

profile of v5, /device:TPU:0, one launch (start us, length us, event | category | flops | bytes accessed | tf_op | source)
XLA Modules:
  0.0 16.7 jit_solution(17123077746045739814)
XLA Ops:
  0.0 16.0 %shard_map.100 = bf16[256,256]{1,0:T(8,128)(2,1)S(1)} custom-call(bf16[256,256]{1,0:T(8,128)(2,1)} %tokens_hbm.1, f32[1,256]{1,0:T(1,128)} %bitcast.2, bf16[256,768]{1,0:T(8,128)(2,1)} %w_in_hbm.1, f32[3,768]{1,0:T(4,128)} %short_hbm.1, f32[256,256]{1,0:T(8,128)} %long_hbm.1, f32[128,256]{1,0:T(8,128)} %med_hbm.1, f32[1,256]{1,0:T(1,128)} %bitcast.3, ...), custom_call_target="tpu_custom_call" | custom-call | tf_op jit(solution)/shard_map/pallas_call | solution.py:490
  16.0 0.7 %copy.12 = bf16[256,256]{1,0:T(8,128)(2,1)} copy(bf16[256,256]{1,0:T(8,128)(2,1)S(1)} %shard_map.100) | data formatting | bytes 262144

commit v6 on v5

--- a/solution.py
+++ b/solution.py
@@ -176,26 +176,6 @@
     near = relative(lax.rem(own, plane), plane)
     far = [plane + x for x in near]
     rim = halo.shape[0]
-    in_back = jnp.logical_not(in_front)
-    barrier = pltpu.get_barrier_semaphore()
-
-    def announce(semaphore, peer):
-        pl.semaphore_signal(
-            semaphore, inc=1, device_id={"seq": peer}, device_id_type=pl.DeviceIdType.MESH
-        )
-
-    @pl.when(in_front)
-    def _():
-        for d in same:
-            announce(barrier, d)
-        for d in cross:
-            announce(barrier, side + d)
-
-    @pl.when(in_back)
-    def _():
-        for d in same:
-            announce(barrier, side + d)
-
     def copies(pairs):
         return [
             pltpu.make_async_copy(source, target, local_sem.at[num])
@@ -212,7 +192,30 @@
         ]
     )
     later_loads = copies([(matrices_hbm, matrices), (w_out_hbm, w_out), (turns_hbm, turns)])
-    for load in loads:
+    for load in loads[:5]:
+        load.start()
+
+    in_back = jnp.logical_not(in_front)
+    barrier = pltpu.get_barrier_semaphore()
+
+    def announce(semaphore, peer):
+        pl.semaphore_signal(
+            semaphore, inc=1, device_id={"seq": peer}, device_id_type=pl.DeviceIdType.MESH
+        )
+
+    @pl.when(in_front)
+    def _():
+        for d in same:
+            announce(barrier, d)
+        for d in cross:
+            announce(barrier, side + d)
+
+    @pl.when(in_back)
+    def _():
+        for d in same[-1:] + same[:-1]:
+            announce(barrier, side + d)
+
+    for load in loads[5:]:
         load.start()
 
     @pl.when(me == devices - 1)

time: 16.8 us -> 16.9 us (level)
  no operation moved by 1% of the time
where the time goes in v6:
time: 16.9 us; the launch traced here: 16.7 us
  Pallas kernels  16 us (95%)
  local copies, waits for them, and re-layouts  0.66 us (4%)
    pallas_call x1, Pallas kernels, fused(): pl.pallas_call(functools.partial(kernel, devices), out_shape=pltpu.VMEM((...  16 us
    unnamed x1, local copies, waits for them, and re-layouts  0.66 us

profile of v6, /device:TPU:0, one launch (start us, length us, event | category | flops | bytes accessed | tf_op | source)
XLA Modules:
  0.0 16.7 jit_solution(4694128222566485524)
XLA Ops:
  0.0 16.0 %shard_map.100 = bf16[256,256]{1,0:T(8,128)(2,1)S(1)} custom-call(bf16[256,256]{1,0:T(8,128)(2,1)} %tokens_hbm.1, f32[1,256]{1,0:T(1,128)} %bitcast.2, bf16[256,768]{1,0:T(8,128)(2,1)} %w_in_hbm.1, f32[3,768]{1,0:T(4,128)} %short_hbm.1, f32[256,256]{1,0:T(8,128)} %long_hbm.1, f32[128,256]{1,0:T(8,128)} %med_hbm.1, f32[1,256]{1,0:T(1,128)} %bitcast.3, ...), custom_call_target="tpu_custom_call" | custom-call | tf_op jit(solution)/shard_map/pallas_call | solution.py:493
  16.0 0.7 %copy.12 = bf16[256,256]{1,0:T(8,128)(2,1)} copy(bf16[256,256]{1,0:T(8,128)(2,1)S(1)} %shard_map.100) | data formatting | bytes 262144

commit v7 on v6

--- a/solution.py
+++ b/solution.py
@@ -307,8 +307,8 @@
             pl.semaphore_wait(barrier, devices - 1)
             halo_copy.start()
 
+        cross_from_back(0)
         same_from_back(0)
-        cross_from_back(0)
 
     for load in loads[2:]:
         load.wait()

time: 16.9 us -> 16.8 us (level)
  no operation moved by 1% of the time
where the time goes in v7:
time: 16.8 us; the launch traced here: 16.7 us
  Pallas kernels  16 us (95%)
  local copies, waits for them, and re-layouts  0.66 us (4%)
    pallas_call x1, Pallas kernels, fused(): pl.pallas_call(functools.partial(kernel, devices), out_shape=pltpu.VMEM((...  16 us
    unnamed x1, local copies, waits for them, and re-layouts  0.66 us

profile of v7, /device:TPU:0, one launch (start us, length us, event | category | flops | bytes accessed | tf_op | source)
XLA Modules:
  0.0 16.7 jit_solution(16909185941032629877)
XLA Ops:
  0.0 16.0 %shard_map.100 = bf16[256,256]{1,0:T(8,128)(2,1)S(1)} custom-call(bf16[256,256]{1,0:T(8,128)(2,1)} %tokens_hbm.1, f32[1,256]{1,0:T(1,128)} %bitcast.2, bf16[256,768]{1,0:T(8,128)(2,1)} %w_in_hbm.1, f32[3,768]{1,0:T(4,128)} %short_hbm.1, f32[256,256]{1,0:T(8,128)} %long_hbm.1, f32[128,256]{1,0:T(8,128)} %med_hbm.1, f32[1,256]{1,0:T(1,128)} %bitcast.3, ...), custom_call_target="tpu_custom_call" | custom-call | tf_op jit(solution)/shard_map/pallas_call | solution.py:493
  16.0 0.7 %copy.12 = bf16[256,256]{1,0:T(8,128)(2,1)} copy(bf16[256,256]{1,0:T(8,128)(2,1)S(1)} %shard_map.100) | data formatting | bytes 262144
